TPU v7x, 32 devices: a whole 2x2x4 slice. The times are simulated.
32 devices in a mesh: fsdp: 2 (over x), context: 16 (over z, y, core).
Axes of the slice: x: 2, y: 2, z: 4, core: 2. Of those that a mesh axis runs over, the one named last changes fastest.
Arguments:
- tokens: bfloat16 [2, 2048, 1600], P('fsdp', 'context'), may hold values from -6 to 6
- cotangent: bfloat16 [2, 2048, 1600], P('fsdp', 'context'), may hold values from -6 to 6
- block_order: int32 [32], replicated, may hold values from 0 to 31, each once
- ln1_gain: bfloat16 [1600], P('fsdp'), may hold values from 0.5 to 1.5
- ln1_bias: bfloat16 [1600], P('fsdp'), may hold values from -3 to 3
- w_qkv: bfloat16 [1600, 4800], P('context', 'fsdp'), may hold values from -5.05 to 5.05
- qv_bias: bfloat16 [1600, 2], P('fsdp'), may hold values from -0.29882812 to 0.29882812
- w_out: bfloat16 [1600, 1600], P('context', 'fsdp'), may hold values from -0.875 to 0.875
- out_bias: bfloat16 [1600], P('fsdp'), may hold values from -3 to 3
- ln2_gain: bfloat16 [1600], P('fsdp'), may hold values from 0.5 to 1.5
- ln2_bias: bfloat16 [1600], P('fsdp'), may hold values from -3 to 3
- w_fc: bfloat16 [1600, 6400], P('context', 'fsdp'), may hold values from -0.15625 to 0.15625
- fc_bias: bfloat16 [6400], P('fsdp'), may hold values from -3 to 3
- w_proj: bfloat16 [6400, 1600], P('context', 'fsdp'), may hold values from -0.078125 to 0.078125
- proj_bias: bfloat16 [1600], P('fsdp'), may hold values from -3 to 3
Outputs:
- out: bfloat16 [2, 2048, 1600], P('fsdp', 'context')
- d_tokens: bfloat16 [2, 2048, 1600], P('fsdp', 'context')
- g_ln1_gain: float32 [1600], P('fsdp')
- g_ln1_bias: float32 [1600], P('fsdp')
- g_w_qkv: float32 [1600, 4800], P('context', 'fsdp')
- g_qv_bias: float32 [1600, 2], P('fsdp')
- g_w_out: float32 [1600, 1600], P('context', 'fsdp')
- g_out_bias: float32 [1600], P('fsdp')
- g_ln2_gain: float32 [1600], P('fsdp')
- g_ln2_bias: float32 [1600], P('fsdp')
- g_w_fc: float32 [1600, 6400], P('context', 'fsdp')
- g_fc_bias: float32 [6400], P('fsdp')
- g_w_proj: float32 [6400, 1600], P('context', 'fsdp')
- g_proj_bias: float32 [1600], P('fsdp')
Inputs may be any that keep to these rules, and one draw needn't show every extreme that they name: block_order names each of the 32 blocks of positions once; rows s * 64 to s * 64 + 63 of a sequence hold positions block_order[s] * 64 onward, in order.
All inputs are finite; a program needn't handle non-finite values.
Results may differ from a plain program's by a relative error of at most 0.025.
Values may be sent and summed in bfloat16 or wider, within the bound.
No kernel may reach another device: no remote copies, remote signals or barrier semaphores. Data moves between devices by JAX's collectives and lax.ppermute only.
A program may use at most 576 MiB of HBM per device.

v0:
```python
import math
import jax
import jax.numpy as jnp
from jax import lax
from jax.sharding import PartitionSpec as P

HEADS = 25
HEAD_DIM = 64
EPSILON = 1e-05
GELU_ROOT = math.sqrt(2.0 / math.pi)
GELU_CUBIC = 0.044715
NEG_LARGE = -1e30


def normalize(values, gain_vec, bias_vec):
    centred = values - jnp.mean(values, axis=-1, keepdims=True)
    inv_std = lax.rsqrt(jnp.mean(centred * centred, axis=-1, keepdims=True) + EPSILON)
    normed = centred * inv_std
    return (normed * gain_vec.astype(jnp.float32) + bias_vec.astype(jnp.float32), normed, inv_std)


def norm_back(upstream, normed, inv_std, gain_vec):
    scaled = upstream * gain_vec.astype(jnp.float32)
    return inv_std * (
        scaled
        - jnp.mean(scaled, axis=-1, keepdims=True)
        - normed * jnp.mean(scaled * normed, axis=-1, keepdims=True)
    )


def gelu_pair(pre_act):
    inner = GELU_ROOT * (pre_act + GELU_CUBIC * pre_act * pre_act * pre_act)
    tangent = jnp.tanh(inner)
    act_value = 0.5 * pre_act * (1.0 + tangent)
    act_slope = 0.5 * (1.0 + tangent) + 0.5 * pre_act * (1.0 - tangent * tangent) * GELU_ROOT * (
        1.0 + 3.0 * GELU_CUBIC * pre_act * pre_act
    )
    return (act_value, act_slope)


def positions_of(block_order, block_len):
    offsets = jnp.arange(block_len, dtype=jnp.int32)
    return (block_order[:, None] * block_len + offsets[None, :]).reshape(-1)


def gather_rows(first, second):
    return (
        lax.all_gather(first, "context", axis=0, tiled=True),
        lax.all_gather(second, "context", axis=0, tiled=True),
    )


def gather_cols(first, second, vec_a, vec_b, vec_c, vec_d):
    return (
        lax.all_gather(first, "fsdp", axis=1, tiled=True),
        lax.all_gather(second, "fsdp", axis=1, tiled=True),
        lax.all_gather(vec_a, "fsdp", axis=0, tiled=True),
        lax.all_gather(vec_b, "fsdp", axis=0, tiled=True),
        lax.all_gather(vec_c, "fsdp", axis=0, tiled=True),
        lax.all_gather(vec_d, "fsdp", axis=0, tiled=True),
    )


def fetch(first, second, vec_a, vec_b, vec_c, vec_d):
    cols = gather_cols(first, second, vec_a, vec_b, vec_c, vec_d)
    rows = gather_rows(cols[0], cols[1])
    return (rows[0], rows[1], cols[2], cols[3], cols[4], cols[5])


def scatter_rows(first, second):
    return (
        lax.psum_scatter(first, "context", scatter_dimension=0, tiled=True),
        lax.psum_scatter(second, "context", scatter_dimension=0, tiled=True),
    )


def scatter_cols(first, second, vec_a, vec_b, vec_c, vec_d):
    return (
        lax.psum_scatter(
            first.astype(jnp.bfloat16), "fsdp", scatter_dimension=1, tiled=True
        ).astype(jnp.float32),
        lax.psum_scatter(
            second.astype(jnp.bfloat16), "fsdp", scatter_dimension=1, tiled=True
        ).astype(jnp.float32),
        lax.psum_scatter(
            vec_a.astype(jnp.bfloat16), "fsdp", scatter_dimension=0, tiled=True
        ).astype(jnp.float32),
        lax.psum_scatter(
            vec_b.astype(jnp.bfloat16), "fsdp", scatter_dimension=0, tiled=True
        ).astype(jnp.float32),
        lax.psum_scatter(
            vec_c.astype(jnp.bfloat16), "fsdp", scatter_dimension=0, tiled=True
        ).astype(jnp.float32),
        lax.psum_scatter(
            vec_d.astype(jnp.bfloat16), "fsdp", scatter_dimension=0, tiled=True
        ).astype(jnp.float32),
    )


def send_grads(first, second, vec_a, vec_b, vec_c, vec_d):
    rows = scatter_rows(first, second)
    return scatter_cols(rows[0], rows[1], vec_a, vec_b, vec_c, vec_d)


def attend_forward(query_heads, keys_all, values_all, query_pos, key_pos):
    length = keys_all.shape[0]
    rows_here = query_heads.shape[0]
    kblock = math.gcd(length, 512)
    nblocks = length // kblock
    score_scale = HEAD_DIM ** (-0.5)
    key_blocks = keys_all.reshape(nblocks, kblock, HEADS, HEAD_DIM)
    value_blocks = values_all.reshape(nblocks, kblock, HEADS, HEAD_DIM)
    pos_blocks = key_pos.reshape(nblocks, kblock)

    def step(carry, inputs):
        maxima, totals, accum = carry
        block_keys, block_values, block_pos = inputs
        scores = (
            jnp.einsum("qhd,khd->hqk", query_heads, block_keys, preferred_element_type=jnp.float32)
            * score_scale
        )
        allowed = (query_pos[:, None] >= block_pos[None, :])[None]
        fresh = jnp.maximum(maxima, jnp.max(jnp.where(allowed, scores, NEG_LARGE), axis=-1))
        exp_terms = jnp.where(allowed, jnp.exp(scores - fresh[..., None]), 0.0)
        decay_factor = jnp.exp(maxima - fresh)
        totals = totals * decay_factor + jnp.sum(exp_terms, axis=-1)
        accum = accum * decay_factor[..., None] + jnp.einsum(
            "hqk,khd->hqd",
            exp_terms.astype(jnp.bfloat16),
            block_values,
            preferred_element_type=jnp.float32,
        )
        return ((fresh, totals, accum), None)

    start_carry = (
        jnp.full((HEADS, rows_here), NEG_LARGE, jnp.float32),
        jnp.zeros((HEADS, rows_here), jnp.float32),
        jnp.zeros((HEADS, rows_here, HEAD_DIM), jnp.float32),
    )
    (maxima, totals, accum), _ = lax.scan(step, start_carry, (key_blocks, value_blocks, pos_blocks))
    attn_out = (accum / totals[..., None]).transpose(1, 0, 2).reshape(rows_here, HEADS * HEAD_DIM)
    return (attn_out.astype(jnp.bfloat16), maxima + jnp.log(totals))


def block_terms(
    query_heads, grad_heads, row_dot, log_norm, query_pos, block_keys, block_values, block_pos
):
    score_scale = HEAD_DIM ** (-0.5)
    scores = (
        jnp.einsum("qhd,khd->hqk", query_heads, block_keys, preferred_element_type=jnp.float32)
        * score_scale
    )
    allowed = (query_pos[:, None] >= block_pos[None, :])[None]
    prob_full = jnp.where(allowed, jnp.exp(scores - log_norm[..., None]), 0.0)
    prob_half = prob_full.astype(jnp.bfloat16)
    value_grad = jnp.einsum(
        "hqk,qhd->khd", prob_half, grad_heads, preferred_element_type=jnp.float32
    )
    dprob = jnp.einsum("qhd,khd->hqk", grad_heads, block_values, preferred_element_type=jnp.float32)
    dscore = (score_scale * prob_full * (dprob - row_dot[..., None])).astype(jnp.bfloat16)
    query_grad = jnp.einsum("hqk,khd->qhd", dscore, block_keys, preferred_element_type=jnp.float32)
    key_grad = jnp.einsum("hqk,qhd->khd", dscore, query_heads, preferred_element_type=jnp.float32)
    return (query_grad, key_grad, value_grad)


def attend_backward(
    query_heads, keys_all, values_all, query_pos, key_pos, log_norm, grad_o16, attn_out
):
    length = keys_all.shape[0]
    rows_here = query_heads.shape[0]
    width = HEADS * HEAD_DIM
    kblock = math.gcd(length, 512)
    nblocks = length // kblock
    grad_heads = grad_o16.reshape(rows_here, HEADS, HEAD_DIM)
    row_dot = jnp.sum(
        grad_o16.astype(jnp.float32).reshape(rows_here, HEADS, HEAD_DIM)
        * attn_out.astype(jnp.float32).reshape(rows_here, HEADS, HEAD_DIM),
        axis=-1,
    ).T
    key_blocks = keys_all.reshape(nblocks, kblock, HEADS, HEAD_DIM)
    value_blocks = values_all.reshape(nblocks, kblock, HEADS, HEAD_DIM)
    pos_blocks = key_pos.reshape(nblocks, kblock)
    start_grad = jnp.zeros((rows_here, HEADS, HEAD_DIM), jnp.float32)

    def step_whole(carry, inputs):
        query_grad, key_grad, value_grad = block_terms(
            query_heads, grad_heads, row_dot, log_norm, query_pos, inputs[0], inputs[1], inputs[2]
        )
        return (carry + query_grad, (key_grad, value_grad))

    query_total, (key_parts, value_parts) = lax.scan(
        step_whole, start_grad, (key_blocks, value_blocks, pos_blocks)
    )
    term = jnp.concatenate(
        [key_parts.reshape(length, width), value_parts.reshape(length, width)], axis=1
    )
    owned = lax.psum_scatter(term, "context", scatter_dimension=0, tiled=True)
    key_owned, value_owned = (owned[:, :width], owned[:, width:])
    return (query_total.reshape(rows_here, width), key_owned, value_owned)


def body(
    tokens,
    cotangent,
    block_order,
    ln1_gain,
    ln1_bias,
    w_qkv,
    qv_bias,
    w_out,
    out_bias,
    ln2_gain,
    ln2_bias,
    w_fc,
    fc_bias,
    w_proj,
    proj_bias,
):
    width = HEADS * HEAD_DIM
    rows_here = tokens.shape[1]
    block_len = rows_here // 2
    grad_scale = 1.0 / math.sqrt(lax.axis_size("fsdp") * lax.axis_size("context") * rows_here)
    key_pos = positions_of(block_order, block_len)
    query_pos = lax.dynamic_slice_in_dim(key_pos, lax.axis_index("context") * rows_here, rows_here)
    w_qkv_all, w_out_all, gain_one, shift_one, qv_all, out_b = fetch(
        w_qkv, w_out, ln1_gain, ln1_bias, qv_bias, out_bias
    )
    w_fc_all, w_proj_all, gain_two, shift_two, fc_b, proj_b = fetch(
        w_fc, w_proj, ln2_gain, ln2_bias, fc_bias, proj_bias
    )
    xs = tokens[0].astype(jnp.float32)
    h_one, normed_one, inv_one = normalize(xs, gain_one, shift_one)
    h_one = h_one.astype(jnp.bfloat16)
    qkv = jnp.dot(h_one, w_qkv_all, preferred_element_type=jnp.float32)
    queries = (qkv[:, :width] + qv_all[:, 0].astype(jnp.float32)).astype(jnp.bfloat16)
    key_rows = qkv[:, width : 2 * width].astype(jnp.bfloat16)
    value_rows = (qkv[:, 2 * width :] + qv_all[:, 1].astype(jnp.float32)).astype(jnp.bfloat16)
    keys_all, values_all = (
        lax.all_gather(key_rows, "context", axis=0, tiled=True),
        lax.all_gather(value_rows, "context", axis=0, tiled=True),
    )
    query_heads = queries.reshape(rows_here, HEADS, HEAD_DIM)
    attn_out, log_norm = attend_forward(query_heads, keys_all, values_all, query_pos, key_pos)
    resid_one = (
        xs
        + jnp.dot(attn_out, w_out_all, preferred_element_type=jnp.float32)
        + out_b.astype(jnp.float32)
    )
    h_two, normed_two, inv_two = normalize(resid_one, gain_two, shift_two)
    h_two = h_two.astype(jnp.bfloat16)
    pre_act = jnp.dot(h_two, w_fc_all, preferred_element_type=jnp.float32) + fc_b.astype(
        jnp.float32
    )
    act_value, act_slope = gelu_pair(pre_act)
    act_half = act_value.astype(jnp.bfloat16)
    result = (
        resid_one
        + jnp.dot(act_half, w_proj_all, preferred_element_type=jnp.float32)
        + proj_b.astype(jnp.float32)
    )
    cot_rows = cotangent[0]
    grad_y = cot_rows.astype(jnp.float32)
    g_w_proj = jnp.dot(act_half.T, cot_rows, preferred_element_type=jnp.float32) * grad_scale
    g_proj_bias = jnp.sum(grad_y, axis=0) * grad_scale
    grad_pre = jnp.dot(cot_rows, w_proj_all.T, preferred_element_type=jnp.float32) * act_slope
    g_fc_bias = jnp.sum(grad_pre, axis=0) * grad_scale
    grad_pre16 = grad_pre.astype(jnp.bfloat16)
    g_w_fc = jnp.dot(h_two.T, grad_pre16, preferred_element_type=jnp.float32) * grad_scale
    grad_h2 = jnp.dot(grad_pre16, w_fc_all.T, preferred_element_type=jnp.float32)
    g_ln2_gain = jnp.sum(grad_h2 * normed_two, axis=0) * grad_scale
    g_ln2_bias = jnp.sum(grad_h2, axis=0) * grad_scale
    mlp_grads = send_grads(g_w_fc, g_w_proj, g_ln2_gain, g_ln2_bias, g_fc_bias, g_proj_bias)
    grad_r1 = grad_y + norm_back(grad_h2, normed_two, inv_two, gain_two)
    g_out_bias = jnp.sum(grad_r1, axis=0) * grad_scale
    grad_r16 = grad_r1.astype(jnp.bfloat16)
    g_w_out = jnp.dot(attn_out.T, grad_r16, preferred_element_type=jnp.float32) * grad_scale
    grad_o16 = jnp.dot(grad_r16, w_out_all.T, preferred_element_type=jnp.float32).astype(
        jnp.bfloat16
    )
    grad_q, grad_k, grad_v = attend_backward(
        query_heads, keys_all, values_all, query_pos, key_pos, log_norm, grad_o16, attn_out
    )
    g_qv_bias = jnp.stack([jnp.sum(grad_q, axis=0), jnp.sum(grad_v, axis=0)], axis=1) * grad_scale
    grad_qkv16 = jnp.concatenate([grad_q, grad_k, grad_v], axis=1).astype(jnp.bfloat16)
    g_w_qkv = jnp.dot(h_one.T, grad_qkv16, preferred_element_type=jnp.float32) * grad_scale
    grad_h1 = jnp.dot(grad_qkv16, w_qkv_all.T, preferred_element_type=jnp.float32)
    g_ln1_gain = jnp.sum(grad_h1 * normed_one, axis=0) * grad_scale
    g_ln1_bias = jnp.sum(grad_h1, axis=0) * grad_scale
    grad_x = (grad_r1 + norm_back(grad_h1, normed_one, inv_one, gain_one)).astype(jnp.bfloat16)
    attn_grads = send_grads(g_w_qkv, g_w_out, g_ln1_gain, g_ln1_bias, g_qv_bias, g_out_bias)
    summed = lax.psum(
        (
            attn_grads[2],
            attn_grads[3],
            attn_grads[4],
            attn_grads[5],
            mlp_grads[2],
            mlp_grads[3],
            mlp_grads[4],
            mlp_grads[5],
        ),
        "context",
    )
    return (
        result.astype(jnp.bfloat16)[None],
        grad_x[None],
        summed[0],
        summed[1],
        attn_grads[0],
        summed[2],
        attn_grads[1],
        summed[3],
        summed[4],
        summed[5],
        mlp_grads[0],
        summed[6],
        mlp_grads[1],
        summed[7],
    )


def solution(mesh):
    placed = (
        P("fsdp", "context", None),
        P("fsdp", "context", None),
        P(),
        P("fsdp"),
        P("fsdp"),
        P("context", "fsdp"),
        P("fsdp", None),
        P("context", "fsdp"),
        P("fsdp"),
        P("fsdp"),
        P("fsdp"),
        P("context", "fsdp"),
        P("fsdp"),
        P("context", "fsdp"),
        P("fsdp"),
    )
    return jax.shard_map(
        body,
        mesh=mesh,
        in_specs=placed,
        out_specs=(
            P("fsdp", "context", None),
            P("fsdp", "context", None),
            P("fsdp"),
            P("fsdp"),
            P("context", "fsdp"),
            P("fsdp", None),
            P("context", "fsdp"),
            P("fsdp"),
            P("fsdp"),
            P("fsdp"),
            P("context", "fsdp"),
            P("fsdp"),
            P("context", "fsdp"),
            P("fsdp"),
        ),
        check_vma=False,
    )
```

profile of v0, /device:TPU:0, one launch (start us, length us, event | category | flops | bytes accessed | tf_op | source)
XLA Modules:
  0.0 2697.7 jit_solution(1883228032706122756)
XLA Ops:
  59.3 110.0 %all-gather.25.cloned.1.call-done = bf16[16,100,4800]{2,1,0:T(8,128)(2,1)} async-done(((bf16[1,100,4800]{2,1,0:T(8,128)(2,1)}), bf16[16,100,4800]{2,1,0:T(8,128)(2,1)}) %all-gather.25.cloned.1.call-update) | async-done | bytes 15360016 | tf_op jit(solution)/shard_map/all_gather | solution.py:48
  212.7 42.3 %all-gather.27.cloned.1.call-done = bf16[16,100,1600]{2,1,0:T(8,128)(2,1)} async-done(((bf16[1,100,1600]{2,1,0:T(8,128)(2,1)}), bf16[16,100,1600]{2,1,0:T(8,128)(2,1)}) %all-gather.27.cloned.1.call-update) | async-done | bytes 5120016 | tf_op jit(solution)/shard_map/all_gather | solution.py:49
  263.2 102.2 %all-gather.29.cloned.1.call-done = bf16[16,100,6400]{2,1,0:T(8,128)(2,1)} async-done(((bf16[1,100,6400]{2,1,0:T(8,128)(2,1)}), bf16[16,100,6400]{2,1,0:T(8,128)(2,1)}) %all-gather.29.cloned.1.call-update) | async-done | bytes 20480016 | tf_op jit(solution)/shard_map/all_gather | solution.py:48
  382.7 52.6 %all-gather.19.cloned.1.call-done = bf16[2048,1600]{0,1:T(8,128)(2,1)} async-done(((bf16[128,1600]{0,1:T(8,128)(2,1)}), bf16[2048,1600]{0,1:T(8,128)(2,1)}) %all-gather.19.cloned.1.call-update) | async-done | bytes 6553616 | tf_op jit(solution)/shard_map/all_gather | solution.py:240
  456.9 46.5 %all-gather.17.cloned.1.call-done = bf16[2048,1600]{0,1:T(8,128)(2,1)} async-done(((bf16[128,1600]{0,1:T(8,128)(2,1)}), bf16[2048,1600]{0,1:T(8,128)(2,1)}) %all-gather.17.cloned.1.call-update) | async-done | bytes 6553616 | tf_op jit(solution)/shard_map/all_gather | solution.py:239
  525.1 31.6 %while.30 = (s32[]{:T(128)}, f32[25,128]{1,0:T(8,128)S(1)}, f32[25,128]{1,0:T(8,128)S(1)}, f32[25,128,64]{1,2,0:T(8,128)S(1)}, s32[128]{0:T(128)S(1)}, /*index=5...) while((s32[]{:T(128)}, f32[25,128]{1,0:T(8,128)S(1)}, ...), condition=%wide.region_5.6_spmd.clone, body=%wide.region_2.5_spmd.clone.sunk | while | flops 438148736 | bytes 25459340 | solution.py:140
  574.5 39.6 %all-gather.23.cloned.1.call-done = bf16[6400,1600]{1,0:T(8,128)(2,1)} async-done(((bf16[400,1600]{1,0:T(8,128)(2,1)}), bf16[6400,1600]{1,0:T(8,128)(2,1)}) %all-gather.23.cloned.1.call-update) | async-done | bytes 20480016 | tf_op jit(solution)/shard_map/all_gather | solution.py:49
  646.3 598.5 %while.31 = (s32[]{:T(128)}, f32[128,25,64]{0,2,1:T(8,128)}, f32[4,512,25,64]{1,0,3,2:T(4,128)}, f32[4,512,25,64]{1,0,3,2:T(4,128)}, bf16[4,512,25,64]{1,3,2,0:T...) while((s32[]{:T(128)}, f32[128,25,64]{0,2,1:T(8,128)}, ...), condition=%wide.region_12.13_spmd.clone, body=%wide.region_11.12_spmd.clone.sunk | while | flops 1067073536 | bytes 77246696 | solution.py:191
  669.9 63.3 %dynamic_update_slice.11 = f32[4,512,25,64]{1,0,3,2:T(4,128)} dynamic-update-slice(f32[4,512,25,64]{1,0,3,2:T(4,128)} %get-tuple-element.552, f32[1,512,25,64]{1,0,3,2:T(1,128)} %copy.106, s32[]{:T(128)S(6)} %copy.132, s32[]{:T(128)} %constant.28.clone.1..sunk.1, s32[]{:T(128)} %constant.28.clone.1..sunk.1, s32[]{:T(128)} %constant.28.clone.1..sunk.1) | dynamic-update-slice | bytes 6553604 | tf_op jit(solution)/shard_map/while/body/jit(dynamic_update_index_in_dim)/dynamic_update_slice | solution.py:191
  733.2 63.0 %dynamic_update_slice.12 = f32[4,512,25,64]{1,0,3,2:T(4,128)} dynamic-update-slice(f32[4,512,25,64]{1,0,3,2:T(4,128)} %get-tuple-element.553, f32[1,512,25,64]{1,0,3,2:T(1,128)S(1)} %copy.107, s32[]{:T(128)S(6)} %copy.132, s32[]{:T(128)} %constant.28.clone.1..sunk.1, s32[]{:T(128)} %constant.28.clone.1..sunk.1, s32[]{:T(128)} %constant.28.clone.1..sunk.1) | dynamic-update-slice | bytes 6553604 | tf_op jit(solution)/shard_map/while/body/jit(dynamic_update_index_in_dim)/dynamic_update_slice | solution.py:191
  819.4 63.3 %dynamic_update_slice.11 = f32[4,512,25,64]{1,0,3,2:T(4,128)} dynamic-update-slice(f32[4,512,25,64]{1,0,3,2:T(4,128)} %get-tuple-element.552, f32[1,512,25,64]{1,0,3,2:T(1,128)} %copy.106, s32[]{:T(128)S(6)} %copy.132, s32[]{:T(128)} %constant.28.clone.1..sunk.1, s32[]{:T(128)} %constant.28.clone.1..sunk.1, s32[]{:T(128)} %constant.28.clone.1..sunk.1) | dynamic-update-slice | bytes 6553604 | tf_op jit(solution)/shard_map/while/body/jit(dynamic_update_index_in_dim)/dynamic_update_slice | solution.py:191
  882.7 63.0 %dynamic_update_slice.12 = f32[4,512,25,64]{1,0,3,2:T(4,128)} dynamic-update-slice(f32[4,512,25,64]{1,0,3,2:T(4,128)} %get-tuple-element.553, f32[1,512,25,64]{1,0,3,2:T(1,128)S(1)} %copy.107, s32[]{:T(128)S(6)} %copy.132, s32[]{:T(128)} %constant.28.clone.1..sunk.1, s32[]{:T(128)} %constant.28.clone.1..sunk.1, s32[]{:T(128)} %constant.28.clone.1..sunk.1) | dynamic-update-slice | bytes 6553604 | tf_op jit(solution)/shard_map/while/body/jit(dynamic_update_index_in_dim)/dynamic_update_slice | solution.py:191
  968.9 63.3 %dynamic_update_slice.11 = f32[4,512,25,64]{1,0,3,2:T(4,128)} dynamic-update-slice(f32[4,512,25,64]{1,0,3,2:T(4,128)} %get-tuple-element.552, f32[1,512,25,64]{1,0,3,2:T(1,128)} %copy.106, s32[]{:T(128)S(6)} %copy.132, s32[]{:T(128)} %constant.28.clone.1..sunk.1, s32[]{:T(128)} %constant.28.clone.1..sunk.1, s32[]{:T(128)} %constant.28.clone.1..sunk.1) | dynamic-update-slice | bytes 6553604 | tf_op jit(solution)/shard_map/while/body/jit(dynamic_update_index_in_dim)/dynamic_update_slice | solution.py:191
  1032.1 63.0 %dynamic_update_slice.12 = f32[4,512,25,64]{1,0,3,2:T(4,128)} dynamic-update-slice(f32[4,512,25,64]{1,0,3,2:T(4,128)} %get-tuple-element.553, f32[1,512,25,64]{1,0,3,2:T(1,128)S(1)} %copy.107, s32[]{:T(128)S(6)} %copy.132, s32[]{:T(128)} %constant.28.clone.1..sunk.1, s32[]{:T(128)} %constant.28.clone.1..sunk.1, s32[]{:T(128)} %constant.28.clone.1..sunk.1) | dynamic-update-slice | bytes 6553604 | tf_op jit(solution)/shard_map/while/body/jit(dynamic_update_index_in_dim)/dynamic_update_slice | solution.py:191
  1118.3 63.3 %dynamic_update_slice.11 = f32[4,512,25,64]{1,0,3,2:T(4,128)} dynamic-update-slice(f32[4,512,25,64]{1,0,3,2:T(4,128)} %get-tuple-element.552, f32[1,512,25,64]{1,0,3,2:T(1,128)} %copy.106, s32[]{:T(128)S(6)} %copy.132, s32[]{:T(128)} %constant.28.clone.1..sunk.1, s32[]{:T(128)} %constant.28.clone.1..sunk.1, s32[]{:T(128)} %constant.28.clone.1..sunk.1) | dynamic-update-slice | bytes 6553604 | tf_op jit(solution)/shard_map/while/body/jit(dynamic_update_index_in_dim)/dynamic_update_slice | solution.py:191
  1181.6 63.0 %dynamic_update_slice.12 = f32[4,512,25,64]{1,0,3,2:T(4,128)} dynamic-update-slice(f32[4,512,25,64]{1,0,3,2:T(4,128)} %get-tuple-element.553, f32[1,512,25,64]{1,0,3,2:T(1,128)S(1)} %copy.107, s32[]{:T(128)S(6)} %copy.132, s32[]{:T(128)} %constant.28.clone.1..sunk.1, s32[]{:T(128)} %constant.28.clone.1..sunk.1, s32[]{:T(128)} %constant.28.clone.1..sunk.1) | dynamic-update-slice | bytes 6553604 | tf_op jit(solution)/shard_map/while/body/jit(dynamic_update_index_in_dim)/dynamic_update_slice | solution.py:191
  1276.9 19.0 pad_maximum_fusion
  1297.6 26.2 convolution_multiply_fusion
  1323.8 507.8 %fusion.2 = f32[104,6400]{1,0:T(8,128)S(1)} fusion(f32[1600,6400]{1,0:T(8,128)} %convolution_multiply_fusion), kind=kCustom, calls=%all-reduce-scatter.2 | all-reduce-scatter fusion | flops 10649601 | bytes 43622912
  1832.6 29.2 %collective-permute-start.3 = (bf16[60,6400]{1,0:T(8,128)(2,1)}, bf16[60,6400]{1,0:T(8,128)(2,1)}, u32[]{:S(2)}, u32[]{:S(2)}) collective-permute-start(bf16[60,6400]{1,0:T(8,128)(2,1)} %slice.35), channel_id=1, source_target_pairs={{0,1},{1,2},{2,3},{3,4},{4,5},{5,6},{6,7},{7,8},{8,9},{9,10},{10,1... | collective-permute-start | bytes 2304008
  1879.1 18.5 convolution_multiply_fusion.1
  1921.7 591.9 %fusion.103 = (f32[104,4800]{1,0:T(8,128)}, f32[112,1600]{1,0:T(8,128)S(1)}) fusion(f32[1600,4800]{1,0:T(8,128)} %convolution_multiply_fusion.2, f32[1600,1600]{1,0:T(8,128)} %convolution_multiply_fusion.3), kind=kCustom, calls=%all-reduce-scatter.3 | all-reduce-scatter fusion | flops 10854402 | bytes 43674112
  2514.4 28.0 %collective-permute-start.1 = (bf16[112,1600]{1,0:T(8,128)(2,1)}, bf16[112,1600]{1,0:T(8,128)(2,1)S(1)}, u32[]{:S(2)}, u32[]{:S(2)}) collective-permute-start(bf16[112,1600]{1,0:T(8,128)(2,1)} %convert.26), channel_id=1, source_target_pairs={{0,1},{1,2},{2,3},{3,4},{4,5},{5,6},{6,7},{7,8},{8,9},{9,10},{10,1... | collective-permute-start | bytes 1075208
  2624.2 59.8 %all-reduce.19 = (f32[800]{0:T(1024)}, f32[800]{0:T(1024)}, f32[800,2]{0,1:T(2,128)}, f32[800]{0:T(1024)}, f32[800]{0:T(1024)}, /*index=5*/f32[800]{0:T(1024)}, f32[3200]{0:T(1024)}, f32[800]{0:T(1024)}) all-reduce(f32[800]{0:T(1024)S(1)} %dynamic-slice_convert_fusion.9, ...), channel_id=1, replica_groups=mesh['fsdp'=2,'context'=16] {'context'}, use_global_device_ids=true, to_apply=%region_18.19 | all-reduce | flops 9600 | bytes 73600 | tf_op jit(solution)/shard_map/psum | solution.py:291
  (349 shorter events, 499.3 us)
Async XLA Ops:
  7.2 35.4 %all-gather.21.cloned.1.call-start = ((), (), s32[]{:S(2)}) async-start(), calls=%async_computation.9 | async-start | bytes 1996800 | tf_op jit(solution)/shard_map/all_gather | solution.py:55
  7.9 161.5 %all-gather.25.cloned.1.call-start = ((), (), s32[]{:S(2)}) async-start(), calls=%async_computation.13 | async-start | bytes 17199104 | tf_op jit(solution)/shard_map/all_gather | solution.py:48
  29.1 173.6 %all-gather.31.cloned.1.call-start = ((), (), s32[]{:S(2)}) async-start(), calls=%async_computation.16 | async-start | bytes 2150400 | tf_op jit(solution)/shard_map/all_gather | solution.py:56
  29.8 225.1 %all-gather.27.cloned.1.call-start = ((), (), s32[]{:S(2)}) async-start(), calls=%async_computation.14 | async-start | bytes 5883904 | tf_op jit(solution)/shard_map/all_gather | solution.py:49
  42.5 323.0 %all-gather.29.cloned.1.call-start = ((), (), s32[]{:S(2)}) async-start(), calls=%async_computation.15 | async-start | bytes 22630400 | tf_op jit(solution)/shard_map/all_gather | solution.py:48
  43.1 392.2 %all-gather.19.cloned.1.call-start = ((), (), s32[]{:S(2)}) async-start(), calls=%async_computation.8 | async-start | bytes 6963200 | tf_op jit(solution)/shard_map/all_gather | solution.py:240
  54.3 131.2 %copy-start.20 = (f32[1600]{0:T(1024)}, f32[1600]{0:T(1024)S(1)}, u32[]{:S(2)}) copy-start(f32[1600]{0:T(1024)S(1)} %convert_element_type.185) | copy-start | bytes 19204
  58.8 126.7 %copy-start.18 = (f32[1600]{0:T(1024)}, f32[1600]{0:T(1024)S(1)}, u32[]{:S(2)}) copy-start(f32[1600]{0:T(1024)S(1)} %convert_element_type.184) | copy-start | bytes 19204
  59.1 126.4 %copy-start.30 = (f32[128]{0:T(128)}, f32[128]{0:T(128)S(1)}, u32[]{:S(2)}) copy-start(f32[128]{0:T(128)S(1)} %broadcast_multiply_fusion.5) | copy-start | bytes 1540
  200.6 302.8 %all-gather.17.cloned.1.call-start = ((), (), s32[]{:S(2)}) async-start(), calls=%async_computation.7 | async-start | bytes 6963200 | tf_op jit(solution)/shard_map/all_gather | solution.py:239
  202.6 411.6 %all-gather.23.cloned.1.call-start = ((), (), s32[]{:S(2)}) async-start(), calls=%async_computation.10 | async-start | bytes 22630400 | tf_op jit(solution)/shard_map/all_gather | solution.py:49
  207.0 1699.5 %reduce-scatter.24.cloned.1.call-start = ((), (), s32[]{:S(2)}) async-start(), calls=%async_computation.11 | async-start | bytes 27852800 | tf_op jit(solution)/shard_map/reduce_scatter | solution.py:197
  207.3 354.8 %copy-start.22 = (f32[1600]{0:T(1024)}, f32[1600]{0:T(1024)S(1)}, u32[]{:S(2)}) copy-start(f32[1600]{0:T(1024)S(1)} %convert_element_type.198) | copy-start | bytes 19204
  1295.9 1267.8 %reduce-scatter.34.cloned.1.call-start = ((), (), s32[]{:S(2)}) async-start(), calls=%async_computation.20 | async-start | bytes 2457600
  1323.8 538.1 %copy-start.43 = (u32[32]{0:T(128)S(1)}, u32[32]{0:T(128)}, u32[]{:S(2)}) copy-start(u32[32]{0:T(128)} %constant.134) | copy-start | bytes 388
  1832.6 30.6 %collective-permute-start.3 = (bf16[60,6400]{1,0:T(8,128)(2,1)}, bf16[60,6400]{1,0:T(8,128)(2,1)}, u32[]{:S(2)}, u32[]{:S(2)}) collective-permute-start(bf16[60,6400]{1,0:T(8,128)(2,1)} %slice.35), channel_id=1, source_target_pairs={{0,1},{1,2},{2,3},{3,4},{4,5},{5,6},{6,7},{7,8},{8,9},{9,10},{10,1... | collective-permute-start | bytes 2304008
  1879.0 721.6 %reduce-scatter.26.cloned.1.call-start = ((), (), s32[]{:S(2)}) async-start(), calls=%async_computation.12 | async-start | bytes 45260800 | tf_op jit(solution)/shard_map/reduce_scatter | solution.py:73
  1897.7 725.5 %reduce-scatter.30.cloned.1.call-start = ((), (), s32[]{:S(2)}) async-start(), calls=%async_computation.18 | async-start | bytes 614400
  2514.4 40.0 %collective-permute-start.1 = (bf16[112,1600]{1,0:T(8,128)(2,1)}, bf16[112,1600]{1,0:T(8,128)(2,1)S(1)}, u32[]{:S(2)}, u32[]{:S(2)}) collective-permute-start(bf16[112,1600]{1,0:T(8,128)(2,1)} %convert.26), channel_id=1, source_target_pairs={{0,1},{1,2},{2,3},{3,4},{4,5},{5,6},{6,7},{7,8},{8,9},{9,10},{10,1... | collective-permute-start | bytes 1075208
  2543.9 10.5 collective-permute-start.2
  2551.0 15.4 collective-permute-start
  2554.3 129.7 %reduce-scatter.32.cloned.1.call-start = ((), (), s32[]{:S(2)}) async-start(), calls=%async_computation.19 | async-start | bytes 614400
  2563.7 122.2 %reduce-scatter.28.cloned.1.call-start = ((), (), s32[]{:S(2)}) async-start(), calls=%async_computation.17 | async-start | bytes 1843200
  2581.1 107.2 %reduce-scatter.36.cloned.1.call-start = ((), (), s32[]{:S(2)}) async-start(), calls=%async_computation.21 | async-start | bytes 2457600
  (46 other events, 597.7 us)
Sparse Core Ops, SparseCore 0:
  9.6 32.3 all-gather.20
  44.8 124.5 all-gather.24
  170.9 23.8 all-gather.30
  197.4 57.5 all-gather.26
  256.4 108.9 all-gather.28
  368.0 67.2 all-gather.18
  438.0 65.3 all-gather.16
  505.6 108.5 all-gather.22
  1296.0 427.5 reduce-scatter.23
  1879.2 37.8 reduce-scatter.33
  1921.9 617.4 reduce-scatter.25
  2554.4 11.3 reduce-scatter.29
  2568.7 13.3 reduce-scatter.31
  2584.2 23.3 reduce-scatter.27
  2609.7 26.7 reduce-scatter.35
where the time goes:
time: 2720 us; the launch traced here: 2700 us
  blocking collectives  1220 us (45%)
  local copies, waits for them, and re-layouts  727 us (27%)
  waiting for transfers between devices  396 us (15%)
  matrix products  229 us (8%)
  starting transfers between devices  65 us (2%)
  other arithmetic  44.6 us (2%)
    unnamed x4, blocking collectives  1120 us
    dynamic_update_slice x16, local copies, waits for them, and re-layouts, attend_backward(): lax.scan(step_whole, start_grad, (key_blocks, value_blocks, pos_blocks))  539 us
    all_gather x2, waiting for transfers between devices, gather_rows(): lax.all_gather(first, 'context', axis=0, tiled=True)  212 us
    unnamed x128, local copies, waits for them, and re-layouts  148 us
    all_gather x2, waiting for transfers between devices, gather_rows(): lax.all_gather(second, 'context', axis=0, tiled=True)  81.9 us
    unnamed x9, starting transfers between devices  64.6 us
    psum x1, blocking collectives, body(): lax.psum((attn_grads[2], attn_grads[3], attn_grads[4], attn_grads[5], mlp...  59.8 us
  transfers between devices with their start and end apart: 19, of which 7 were waited for; matrix products, arithmetic and copies ran while one was open for 52% of the time, Pallas kernels for 0%

commit v1 on v0

--- a/solution.py
+++ b/solution.py
@@ -12,6 +12,27 @@
 NEG_LARGE = -1e30
 
 
+def collect(x, axis, dim):
+    peers, index, width = (lax.axis_size(axis), lax.axis_index(axis), x.shape[dim])
+    right = [(i, (i + 1) % peers) for i in range(peers)]
+    left = [(i, (i - 1) % peers) for i in range(peers)]
+    out = jnp.zeros((*x.shape[:dim], peers * width, *x.shape[dim + 1 :]), x.dtype)
+    out = lax.dynamic_update_slice_in_dim(out, x, index * width, axis=dim)
+    from_left = from_right = x
+    middle = peers // 2
+    for turn in range(1, middle + 1):
+        from_left = lax.ppermute(from_left, axis, right)
+        out = lax.dynamic_update_slice_in_dim(
+            out, from_left, (index - turn) % peers * width, axis=dim
+        )
+        if turn < peers - middle:
+            from_right = lax.ppermute(from_right, axis, left)
+            out = lax.dynamic_update_slice_in_dim(
+                out, from_right, (index + turn) % peers * width, axis=dim
+            )
+    return out
+
+
 def normalize(values, gain_vec, bias_vec):
     centred = values - jnp.mean(values, axis=-1, keepdims=True)
     inv_std = lax.rsqrt(jnp.mean(centred * centred, axis=-1, keepdims=True) + EPSILON)
@@ -44,10 +65,7 @@
 
 
 def gather_rows(first, second):
-    return (
-        lax.all_gather(first, "context", axis=0, tiled=True),
-        lax.all_gather(second, "context", axis=0, tiled=True),
-    )
+    return (lax.all_gather(first, "context", axis=0, tiled=True), collect(second, "context", 0))
 
 
 def gather_cols(first, second, vec_a, vec_b, vec_c, vec_d):

time: 2720 us -> 2900 us (1.066)
  starting transfers between devices: 65 us -> 293 us
  waiting for transfers between devices: 396 us -> 257 us
  local copies, waits for them, and re-layouts: 727 us -> 798 us
    ppermute x0 -> x30, starting transfers between devices: none -> 222 us  [the longest x16 192 us: collect(): from_left = lax.ppermute(from_left, axis, right)]
    ppermute x0 -> x30, waiting for transfers between devices: none -> 126 us  [the longest x16 96.9 us: collect(): from_left = lax.ppermute(from_left, axis, right)]
    all_gather x2, waiting for transfers between devices: 212 us -> 116 us  [gather_rows(): lax.all_gather(first, 'context', axis=0, tiled=True)]
    all_gather x2 -> x0, waiting for transfers between devices: 81.9 us -> none  [gather_rows(): lax.all_gather(second, 'context', axis=0, tiled=True)]
    dynamic_update_slice x0 -> x32, local copies, waits for them, and re-layouts: none -> 77.2 us  [the longest x16 38 us: collect(): lax.dynamic_update_slice_in_dim(out, from_left, (index - turn) % peers *...]
    all_gather x1, waiting for transfers between devices: 52.6 us -> 0.01 us  [body(): lax.all_gather(value_rows, 'context', axis=0, tiled=True)]
    all_gather x1, waiting for transfers between devices: 46.5 us -> 0.01 us  [body(): lax.all_gather(key_rows, 'context', axis=0, tiled=True)]
    unnamed x128 -> x161, local copies, waits for them, and re-layouts: 148 us -> 139 us
  transfers between devices with their start and end apart: 19 -> 47, of which waited for: 7 -> 14; matrix products, arithmetic and copies ran while one was open for 52% -> 49% of each run, Pallas kernels for 0% -> 0%
where the time goes in v1:
time: 2900 us; the launch traced here: 2870 us
  blocking collectives  1200 us (41%)
  local copies, waits for them, and re-layouts  798 us (28%)
  starting transfers between devices  293 us (10%)
  waiting for transfers between devices  257 us (9%)
  matrix products  248 us (9%)
  other arithmetic  54.3 us (2%)
    unnamed x4, blocking collectives  1100 us
    dynamic_update_slice x16, local copies, waits for them, and re-layouts, attend_backward(): lax.scan(step_whole, start_grad, (key_blocks, value_blocks, pos_blocks))  532 us
    ppermute x16, starting transfers between devices, collect(): from_left = lax.ppermute(from_left, axis, right)  192 us
    unnamed x161, local copies, waits for them, and re-layouts  139 us
    all_gather x2, waiting for transfers between devices, gather_rows(): lax.all_gather(first, 'context', axis=0, tiled=True)  116 us
    ppermute x16, waiting for transfers between devices, collect(): from_left = lax.ppermute(from_left, axis, right)  96.9 us
    unnamed x9, starting transfers between devices  70.8 us
    psum x1, blocking collectives, body(): lax.psum((attn_grads[2], attn_grads[3], attn_grads[4], attn_grads[5], mlp...  61.2 us
  transfers between devices with their start and end apart: 47, of which 14 were waited for; matrix products, arithmetic and copies ran while one was open for 49% of the time, Pallas kernels for 0%

profile of v1, /device:TPU:0, one launch (start us, length us, event | category | flops | bytes accessed | tf_op | source)
XLA Modules:
  0.0 2871.0 jit_solution(3546585873264735909)
XLA Ops:
  49.5 115.8 %all-gather.20.cloned.1.call-done = bf16[16,100,4800]{2,1,0:T(8,128)(2,1)} async-done(((bf16[1,100,4800]{2,1,0:T(8,128)(2,1)}), bf16[16,100,4800]{2,1,0:T(8,128)(2,1)}) %all-gather.20.cloned.1.call-update) | async-done | bytes 15360016 | tf_op jit(solution)/shard_map/all_gather | solution.py:68
  206.9 44.0 %collective-permute-done.15 = bf16[400,1600]{1,0:T(8,128)(2,1)S(1)} collective-permute-done((bf16[400,1600]{1,0:T(8,128)(2,1)S(1)}, bf16[400,1600]{1,0:T(8,128)(2,1)S(1)}, u32[]{:S(2)}, u32[]{:S(2)}) %collective-permute-start.15) | collective-permute-done | bytes 1280032 | tf_op jit(solution)/shard_map/ppermute | solution.py:24
  264.6 23.2 collective-permute-done.17
  287.8 46.3 %collective-permute-start.19 = (bf16[400,1600]{1,0:T(8,128)(2,1)S(1)}, bf16[400,1600]{1,0:T(8,128)(2,1)}, u32[]{:S(2)}, u32[]{:S(2)}) collective-permute-start(bf16[400,1600]{1,0:T(8,128)(2,1)S(1)} %collective-permute-done.17), channel_id=1, source_target_pairs={{0,1},{1,2},{2,3},{3,4},{4,5},{5,6},{6,7},{7,8},{8,9},{9,10},{10,1... | collective-permute-start | bytes 3840008 | tf_op jit(solution)/shard_map/ppermute | solution.py:24
  336.8 46.6 %collective-permute-start.21 = (bf16[400,1600]{1,0:T(8,128)(2,1)}, bf16[400,1600]{1,0:T(8,128)(2,1)}, u32[]{:S(2)}, u32[]{:S(2)}) collective-permute-start(bf16[400,1600]{1,0:T(8,128)(2,1)} %collective-permute-done.19), channel_id=1, source_target_pairs={{0,1},{1,2},{2,3},{3,4},{4,5},{5,6},{6,7},{7,8},{8,9},{9,10},{10,1... | collective-permute-start | bytes 3840008 | tf_op jit(solution)/shard_map/ppermute | solution.py:24
  469.0 27.9 collective-permute-start.10
  633.7 19.3 collective-permute-done.29
  714.8 55.1 %while.30 = (s32[]{:T(128)}, f32[25,128]{1,0:T(8,128)S(1)}, f32[25,128]{1,0:T(8,128)S(1)}, f32[25,128,64]{1,2,0:T(8,128)S(1)}, s32[128]{0:T(128)S(1)}, /*index=5...) while((s32[]{:T(128)}, f32[25,128]{1,0:T(8,128)S(1)}, ...), condition=%wide.region_5.6_spmd.clone, body=%wide.region_2.5_spmd.clone.sunk | while | flops 438148736 | bytes 51673768 | solution.py:158
  818.1 604.4 %while.31 = (s32[]{:T(128)}, f32[128,25,64]{0,2,1:T(8,128)}, f32[4,512,25,64]{1,0,3,2:T(4,128)}, f32[4,512,25,64]{1,0,3,2:T(4,128)}, bf16[4,512,25,64]{1,3,2,0:T...) while((s32[]{:T(128)}, f32[128,25,64]{0,2,1:T(8,128)}, ...), condition=%wide.region_12.13_spmd.clone, body=%wide.region_11.12_spmd.clone.sunk | while | flops 1067073536 | bytes 98545896 | solution.py:209
  835.2 63.0 %dynamic_update_slice.155 = f32[4,512,25,64]{1,0,3,2:T(4,128)} dynamic-update-slice(f32[4,512,25,64]{1,0,3,2:T(4,128)} %get-tuple-element.552, f32[1,512,25,64]{1,0,3,2:T(1,128)S(1)} %copy.106, s32[]{:T(128)S(6)} %copy.164, s32[]{:T(128)} %constant.186.clone.1..sunk.1, s32[]{:T(128)} %constant.186.clone.1..sunk.1, s32[]{:T(128)} %constant.186.clone.1..sunk.1) | dynamic-update-slice | bytes 6553604 | tf_op jit(solution)/shard_map/while/body/jit(dynamic_update_index_in_dim)/dynamic_update_slice | solution.py:209
  906.0 63.0 %dynamic_update_slice.156 = f32[4,512,25,64]{1,0,3,2:T(4,128)} dynamic-update-slice(f32[4,512,25,64]{1,0,3,2:T(4,128)} %get-tuple-element.553, f32[1,512,25,64]{1,0,3,2:T(1,128)S(1)} %copy.107, s32[]{:T(128)S(6)} %copy.164, s32[]{:T(128)} %constant.186.clone.1..sunk.1, s32[]{:T(128)} %constant.186.clone.1..sunk.1, s32[]{:T(128)} %constant.186.clone.1..sunk.1) | dynamic-update-slice | bytes 6553604 | tf_op jit(solution)/shard_map/while/body/jit(dynamic_update_index_in_dim)/dynamic_update_slice | solution.py:209
  986.2 63.0 %dynamic_update_slice.155 = f32[4,512,25,64]{1,0,3,2:T(4,128)} dynamic-update-slice(f32[4,512,25,64]{1,0,3,2:T(4,128)} %get-tuple-element.552, f32[1,512,25,64]{1,0,3,2:T(1,128)S(1)} %copy.106, s32[]{:T(128)S(6)} %copy.164, s32[]{:T(128)} %constant.186.clone.1..sunk.1, s32[]{:T(128)} %constant.186.clone.1..sunk.1, s32[]{:T(128)} %constant.186.clone.1..sunk.1) | dynamic-update-slice | bytes 6553604 | tf_op jit(solution)/shard_map/while/body/jit(dynamic_update_index_in_dim)/dynamic_update_slice | solution.py:209
  1057.0 63.0 %dynamic_update_slice.156 = f32[4,512,25,64]{1,0,3,2:T(4,128)} dynamic-update-slice(f32[4,512,25,64]{1,0,3,2:T(4,128)} %get-tuple-element.553, f32[1,512,25,64]{1,0,3,2:T(1,128)S(1)} %copy.107, s32[]{:T(128)S(6)} %copy.164, s32[]{:T(128)} %constant.186.clone.1..sunk.1, s32[]{:T(128)} %constant.186.clone.1..sunk.1, s32[]{:T(128)} %constant.186.clone.1..sunk.1) | dynamic-update-slice | bytes 6553604 | tf_op jit(solution)/shard_map/while/body/jit(dynamic_update_index_in_dim)/dynamic_update_slice | solution.py:209
  1137.2 63.0 %dynamic_update_slice.155 = f32[4,512,25,64]{1,0,3,2:T(4,128)} dynamic-update-slice(f32[4,512,25,64]{1,0,3,2:T(4,128)} %get-tuple-element.552, f32[1,512,25,64]{1,0,3,2:T(1,128)S(1)} %copy.106, s32[]{:T(128)S(6)} %copy.164, s32[]{:T(128)} %constant.186.clone.1..sunk.1, s32[]{:T(128)} %constant.186.clone.1..sunk.1, s32[]{:T(128)} %constant.186.clone.1..sunk.1) | dynamic-update-slice | bytes 6553604 | tf_op jit(solution)/shard_map/while/body/jit(dynamic_update_index_in_dim)/dynamic_update_slice | solution.py:209
  1208.0 63.0 %dynamic_update_slice.156 = f32[4,512,25,64]{1,0,3,2:T(4,128)} dynamic-update-slice(f32[4,512,25,64]{1,0,3,2:T(4,128)} %get-tuple-element.553, f32[1,512,25,64]{1,0,3,2:T(1,128)S(1)} %copy.107, s32[]{:T(128)S(6)} %copy.164, s32[]{:T(128)} %constant.186.clone.1..sunk.1, s32[]{:T(128)} %constant.186.clone.1..sunk.1, s32[]{:T(128)} %constant.186.clone.1..sunk.1) | dynamic-update-slice | bytes 6553604 | tf_op jit(solution)/shard_map/while/body/jit(dynamic_update_index_in_dim)/dynamic_update_slice | solution.py:209
  1288.3 63.0 %dynamic_update_slice.155 = f32[4,512,25,64]{1,0,3,2:T(4,128)} dynamic-update-slice(f32[4,512,25,64]{1,0,3,2:T(4,128)} %get-tuple-element.552, f32[1,512,25,64]{1,0,3,2:T(1,128)S(1)} %copy.106, s32[]{:T(128)S(6)} %copy.164, s32[]{:T(128)} %constant.186.clone.1..sunk.1, s32[]{:T(128)} %constant.186.clone.1..sunk.1, s32[]{:T(128)} %constant.186.clone.1..sunk.1) | dynamic-update-slice | bytes 6553604 | tf_op jit(solution)/shard_map/while/body/jit(dynamic_update_index_in_dim)/dynamic_update_slice | solution.py:209
  1359.0 63.0 %dynamic_update_slice.156 = f32[4,512,25,64]{1,0,3,2:T(4,128)} dynamic-update-slice(f32[4,512,25,64]{1,0,3,2:T(4,128)} %get-tuple-element.553, f32[1,512,25,64]{1,0,3,2:T(1,128)S(1)} %copy.107, s32[]{:T(128)S(6)} %copy.164, s32[]{:T(128)} %constant.186.clone.1..sunk.1, s32[]{:T(128)} %constant.186.clone.1..sunk.1, s32[]{:T(128)} %constant.186.clone.1..sunk.1) | dynamic-update-slice | bytes 6553604 | tf_op jit(solution)/shard_map/while/body/jit(dynamic_update_index_in_dim)/dynamic_update_slice | solution.py:209
  1454.7 19.0 pad_maximum_fusion
  1475.3 25.5 convolution_multiply_fusion
  1500.8 498.1 %fusion.2 = f32[104,6400]{1,0:T(8,128)S(1)} fusion(f32[1600,6400]{1,0:T(8,128)} %convolution_multiply_fusion), kind=kCustom, calls=%all-reduce-scatter.2 | all-reduce-scatter fusion | flops 10649601 | bytes 43622912
  1999.9 28.4 collective-permute-start.33
  2087.6 585.4 %fusion.104 = (f32[104,4800]{1,0:T(8,128)}, f32[112,1600]{1,0:T(8,128)S(1)}) fusion(f32[1600,4800]{1,0:T(8,128)} %convolution_multiply_fusion.2, f32[1600,1600]{1,0:T(8,128)} %convolution_multiply_fusion.3), kind=kCustom, calls=%all-reduce-scatter.3 | all-reduce-scatter fusion | flops 10854402 | bytes 43674112
  2673.8 35.0 %collective-permute-start.31 = (bf16[112,1600]{1,0:T(8,128)(2,1)}, bf16[112,1600]{1,0:T(8,128)(2,1)S(1)}, u32[]{:S(2)}, u32[]{:S(2)}) collective-permute-start(bf16[112,1600]{1,0:T(8,128)(2,1)} %convert.26), channel_id=1, source_target_pairs={{0,1},{1,2},{2,3},{3,4},{4,5},{5,6},{6,7},{7,8},{8,9},{9,10},{10,1... | collective-permute-start | bytes 1075208
  2795.8 61.2 %all-reduce.19 = (f32[800]{0:T(1024)}, f32[800]{0:T(1024)}, f32[800,2]{0,1:T(2,128)}, f32[800]{0:T(1024)}, f32[800]{0:T(1024)}, /*index=5*/f32[800]{0:T(1024)}, f32[3200]{0:T(1024)}, f32[800]{0:T(1024)}) all-reduce(f32[800]{0:T(1024)S(1)} %dynamic-slice_convert_fusion.9, ...), channel_id=1, replica_groups=mesh['fsdp'=2,'context'=16] {'context'}, use_global_device_ids=true, to_apply=%region_18.19 | all-reduce | flops 9600 | bytes 73600 | tf_op jit(solution)/shard_map/psum | solution.py:309
  (479 shorter events, 770.6 us)
Async XLA Ops:
  8.0 157.3 %all-gather.20.cloned.1.call-start = ((), (), s32[]{:S(2)}) async-start(), calls=%async_computation.12 | async-start | bytes 17199104 | tf_op jit(solution)/shard_map/all_gather | solution.py:68
  28.8 170.0 %all-gather.24.cloned.1.call-start = ((), (), s32[]{:S(2)}) async-start(), calls=%async_computation.14 | async-start | bytes 2150400 | tf_op jit(solution)/shard_map/all_gather | solution.py:74
  29.6 624.7 %all-gather.22.cloned.1.call-start = ((), (), s32[]{:S(2)}) async-start(), calls=%async_computation.13 | async-start | bytes 22630400 | tf_op jit(solution)/shard_map/all_gather | solution.py:68
  38.0 633.5 %all-gather.14.cloned.1.call-start = ((), (), s32[]{:S(2)}) async-start(), calls=%async_computation.7 | async-start | bytes 6963200 | tf_op jit(solution)/shard_map/all_gather | solution.py:257
  192.8 500.3 %all-gather.16.cloned.1.call-start = ((), (), s32[]{:S(2)}) async-start(), calls=%async_computation.8 | async-start | bytes 6963200 | tf_op jit(solution)/shard_map/all_gather | solution.py:258
  198.8 1873.7 %reduce-scatter.24.cloned.1.call-start = ((), (), s32[]{:S(2)}) async-start(), calls=%async_computation.10 | async-start | bytes 27852800 | tf_op jit(solution)/shard_map/reduce_scatter | solution.py:215
  202.4 48.5 %collective-permute-start.15 = (bf16[400,1600]{1,0:T(8,128)(2,1)S(1)}, bf16[400,1600]{1,0:T(8,128)(2,1)S(1)}, u32[]{:S(2)}, u32[]{:S(2)}) collective-permute-start(bf16[400,1600]{1,0:T(8,128)(2,1)S(1)} %bitcast.264), channel_id=1, source_target_pairs={{0,1},{1,2},{2,3},{3,4},{4,5},{5,6},{6,7},{7,8},{8,9},{9,10},{10,1... | collective-permute-start | bytes 3840008 | tf_op jit(solution)/shard_map/ppermute | solution.py:24
  202.5 62.0 %collective-permute-start.16 = (bf16[400,1600]{1,0:T(8,128)(2,1)S(1)}, bf16[400,1600]{1,0:T(8,128)(2,1)S(1)}, u32[]{:S(2)}, u32[]{:S(2)}) collective-permute-start(bf16[400,1600]{1,0:T(8,128)(2,1)S(1)} %bitcast.265), channel_id=1, source_target_pairs={{0,15},{1,0},{2,1},{3,2},{4,3},{5,4},{6,5},{7,6},{8,7},{9,8},{10,9... | collective-permute-start | bytes 3840008 | tf_op jit(solution)/shard_map/ppermute | solution.py:29
  264.5 69.5 %collective-permute-start.18 = (bf16[400,1600]{1,0:T(8,128)(2,1)S(1)}, bf16[400,1600]{1,0:T(8,128)(2,1)}, u32[]{:S(2)}, u32[]{:S(2)}) collective-permute-start(bf16[400,1600]{1,0:T(8,128)(2,1)S(1)} %collective-permute-done.16), channel_id=1, source_target_pairs={{0,15},{1,0},{2,1},{3,2},{4,3},{5,4},{6,5},{7,6},{8,7},{9,8},{10,9... | collective-permute-start | bytes 3840008 | tf_op jit(solution)/shard_map/ppermute | solution.py:29
  287.8 49.1 %collective-permute-start.19 = (bf16[400,1600]{1,0:T(8,128)(2,1)S(1)}, bf16[400,1600]{1,0:T(8,128)(2,1)}, u32[]{:S(2)}, u32[]{:S(2)}) collective-permute-start(bf16[400,1600]{1,0:T(8,128)(2,1)S(1)} %collective-permute-done.17), channel_id=1, source_target_pairs={{0,1},{1,2},{2,3},{3,4},{4,5},{5,6},{6,7},{7,8},{8,9},{9,10},{10,1... | collective-permute-start | bytes 3840008 | tf_op jit(solution)/shard_map/ppermute | solution.py:24
  334.0 102.6 %collective-permute-start.20 = (bf16[400,1600]{1,0:T(8,128)(2,1)}, bf16[400,1600]{1,0:T(8,128)(2,1)}, u32[]{:S(2)}, u32[]{:S(2)}) collective-permute-start(bf16[400,1600]{1,0:T(8,128)(2,1)} %collective-permute-done.18), channel_id=1, source_target_pairs={{0,15},{1,0},{2,1},{3,2},{4,3},{5,4},{6,5},{7,6},{8,7},{9,8},{10,9... | collective-permute-start | bytes 3840008 | tf_op jit(solution)/shard_map/ppermute | solution.py:29
  336.8 99.8 %collective-permute-start.21 = (bf16[400,1600]{1,0:T(8,128)(2,1)}, bf16[400,1600]{1,0:T(8,128)(2,1)}, u32[]{:S(2)}, u32[]{:S(2)}) collective-permute-start(bf16[400,1600]{1,0:T(8,128)(2,1)} %collective-permute-done.19), channel_id=1, source_target_pairs={{0,1},{1,2},{2,3},{3,4},{4,5},{5,6},{6,7},{7,8},{8,9},{9,10},{10,1... | collective-permute-start | bytes 3840008 | tf_op jit(solution)/shard_map/ppermute | solution.py:24
  436.7 95.9 %collective-permute-start.22 = (bf16[400,1600]{1,0:T(8,128)(2,1)}, bf16[400,1600]{1,0:T(8,128)(2,1)}, u32[]{:S(2)}, u32[]{:S(2)}) collective-permute-start(bf16[400,1600]{1,0:T(8,128)(2,1)} %collective-permute-done.20), channel_id=1, source_target_pairs={{0,15},{1,0},{2,1},{3,2},{4,3},{5,4},{6,5},{7,6},{8,7},{9,8},{10,9... | collective-permute-start | bytes 3840008 | tf_op jit(solution)/shard_map/ppermute | solution.py:29
  436.7 100.3 %collective-permute-start.23 = (bf16[400,1600]{1,0:T(8,128)(2,1)}, bf16[400,1600]{1,0:T(8,128)(2,1)}, u32[]{:S(2)}, u32[]{:S(2)}) collective-permute-start(bf16[400,1600]{1,0:T(8,128)(2,1)} %collective-permute-done.21), channel_id=1, source_target_pairs={{0,1},{1,2},{2,3},{3,4},{4,5},{5,6},{6,7},{7,8},{8,9},{9,10},{10,1... | collective-permute-start | bytes 3840008 | tf_op jit(solution)/shard_map/ppermute | solution.py:24
  532.5 44.0 %collective-permute-start.24 = (bf16[400,1600]{1,0:T(8,128)(2,1)}, bf16[400,1600]{1,0:T(8,128)(2,1)}, u32[]{:S(2)}, u32[]{:S(2)}) collective-permute-start(bf16[400,1600]{1,0:T(8,128)(2,1)} %collective-permute-done.22), channel_id=1, source_target_pairs={{0,15},{1,0},{2,1},{3,2},{4,3},{5,4},{6,5},{7,6},{8,7},{9,8},{10,9... | collective-permute-start | bytes 3840008 | tf_op jit(solution)/shard_map/ppermute | solution.py:29
  537.0 46.6 %collective-permute-start.25 = (bf16[400,1600]{1,0:T(8,128)(2,1)}, bf16[400,1600]{1,0:T(8,128)(2,1)}, u32[]{:S(2)}, u32[]{:S(2)}) collective-permute-start(bf16[400,1600]{1,0:T(8,128)(2,1)} %collective-permute-done.23), channel_id=1, source_target_pairs={{0,1},{1,2},{2,3},{3,4},{4,5},{5,6},{6,7},{7,8},{8,9},{9,10},{10,1... | collective-permute-start | bytes 3840008 | tf_op jit(solution)/shard_map/ppermute | solution.py:24
  610.9 42.1 %collective-permute-start.29 = (bf16[400,1600]{1,0:T(8,128)(2,1)S(1)}, bf16[400,1600]{1,0:T(8,128)(2,1)S(1)}, u32[]{:S(2)}, u32[]{:S(2)}) collective-permute-start(bf16[400,1600]{1,0:T(8,128)(2,1)S(1)} %collective-permute-done.27), channel_id=1, source_target_pairs={{0,1},{1,2},{2,3},{3,4},{4,5},{5,6},{6,7},{7,8},{8,9},{9,10},{10,1... | collective-permute-start | bytes 3840008 | tf_op jit(solution)/shard_map/ppermute | solution.py:24
  1473.7 1261.0 %reduce-scatter.34.cloned.1.call-start = ((), (), s32[]{:S(2)}) async-start(), calls=%async_computation.18 | async-start | bytes 2457600
  2045.4 726.7 %reduce-scatter.26.cloned.1.call-start = ((), (), s32[]{:S(2)}) async-start(), calls=%async_computation.11 | async-start | bytes 45260800 | tf_op jit(solution)/shard_map/reduce_scatter | solution.py:91
  2063.7 731.0 %reduce-scatter.30.cloned.1.call-start = ((), (), s32[]{:S(2)}) async-start(), calls=%async_computation.16 | async-start | bytes 614400
  2673.8 51.5 %collective-permute-start.31 = (bf16[112,1600]{1,0:T(8,128)(2,1)}, bf16[112,1600]{1,0:T(8,128)(2,1)S(1)}, u32[]{:S(2)}, u32[]{:S(2)}) collective-permute-start(bf16[112,1600]{1,0:T(8,128)(2,1)} %convert.26), channel_id=1, source_target_pairs={{0,1},{1,2},{2,3},{3,4},{4,5},{5,6},{6,7},{7,8},{8,9},{9,10},{10,1... | collective-permute-start | bytes 1075208
  2720.8 136.3 %reduce-scatter.32.cloned.1.call-start = ((), (), s32[]{:S(2)}) async-start(), calls=%async_computation.17 | async-start | bytes 614400
  2734.6 124.3 %reduce-scatter.28.cloned.1.call-start = ((), (), s32[]{:S(2)}) async-start(), calls=%async_computation.15 | async-start | bytes 1843200
  2752.1 109.2 %reduce-scatter.36.cloned.1.call-start = ((), (), s32[]{:S(2)}) async-start(), calls=%async_computation.19 | async-start | bytes 2457600
  (95 other events, 4046.2 us)
Sparse Core Ops, SparseCore 0:
  9.6 28.2 all-gather.17
  40.7 124.5 all-gather.19
  166.9 23.8 all-gather.23
  192.2 215.2 all-gather.21
  410.0 101.8 all-gather.13
  514.5 114.1 all-gather.15
  1473.8 427.2 reduce-scatter.23
  2045.5 39.3 reduce-scatter.33
  2089.6 623.3 reduce-scatter.25
  2720.9 12.6 reduce-scatter.29
  2736.4 16.1 reduce-scatter.31
  2754.8 25.2 reduce-scatter.27
  2782.4 26.5 reduce-scatter.35
